TPU v7x, 32 devices: a whole 2x2x4 slice. The times are simulated.
32 devices in a mesh: ctx: 8 (over y, x, core), tp: 4 (over z).
Axes of the slice: x: 2, y: 2, z: 4, core: 2. Of those that a mesh axis runs over, the one named last changes fastest.
Arguments:
- queries: bfloat16 [2048, 8192], P('ctx', 'tp'), may hold values from -22 to 22
- keys: bfloat16 [2048, 512], P('ctx'), may hold values from -22 to 22
- values: bfloat16 [2048, 512], P('ctx'), may hold values from -6 to 6
- grad_out: bfloat16 [2048, 8192], P('ctx', 'tp'), may hold values from -6 to 6
- doc_lengths: int32 [4], replicated, may hold values from 1 to 1024, 2048 in all
Outputs:
- grad_queries: bfloat16 [2048, 8192], P('ctx', 'tp')
- keys_gradient: bfloat16 [2048, 512], P(('ctx', 'tp'))
- values_gradient: bfloat16 [2048, 512], P(('ctx', 'tp'))
Inputs may be any that keep to these rules, and one draw needn't show every extreme that they name: `doc_lengths`: they sum to 2048; the longest is exactly 1024.
All inputs are finite; a program needn't handle non-finite values.
Results may differ from a plain program's by a relative error of at most 0.012.
The roundings to bfloat16 on the way count: a program that leaves them out, or rounds other values in their place, can miss the bound.
Values may be sent and summed in bfloat16 or wider, within the bound.
A program may use at most 192 MiB of HBM per device.

v0:
```python
import jax
import jax.numpy as jnp
from jax import lax
from jax.sharding import PartitionSpec as P

KV_HEAD_COUNT = 4
HEAD_SIZE = 128
QUERY_PER_KV = 16
REACH = 4


NEG = -1e30


def doc_pos(doc_lengths, first, item_count):
    starts = jnp.cumsum(doc_lengths) - doc_lengths
    tok = first + jnp.arange(item_count, dtype=jnp.int32)
    before = starts[None, :] <= tok[:, None]
    docid = jnp.sum(before.astype(jnp.int32), axis=1) - 1
    onehot = docid[:, None] == jnp.arange(starts.shape[0], dtype=jnp.int32)[None, :]
    start_of = jnp.sum(jnp.where(onehot, starts[None, :], 0), axis=1)
    return (tok, docid, tok - start_of)


def rope_tables(pos):
    half = HEAD_SIZE // 2
    freq = 500000.0 ** (-(2.0 * jnp.arange(half, dtype=jnp.float32)) / HEAD_SIZE)
    angle = pos.astype(jnp.float32)[:, None] * freq[None, :]
    return (jnp.cos(angle), jnp.sin(angle))


def apply_rotary(x, cosine_table, sine_table):
    half = HEAD_SIZE // 2
    first, second = (x[..., :half], x[..., half:])
    c, s = (cosine_table[:, None, :], sine_table[:, None, :])
    return jnp.concatenate([first * c - second * s, second * c + first * s], axis=-1)


def invert_rotary(y, cosine_table, sine_table):
    half = HEAD_SIZE // 2
    first, second = (y[..., :half], y[..., half:])
    c, s = (cosine_table[:, None, :], sine_table[:, None, :])
    return jnp.concatenate([first * c + second * s, second * c - first * s], axis=-1)


def local(queries, keys, values, grad_out, doc_lengths):
    token_length = queries.shape[0]
    heads = queries.shape[1] // HEAD_SIZE
    n_ctx = lax.axis_size("ctx")
    n_tp = lax.axis_size("tp")
    ctx_at = lax.axis_index("ctx")
    tp_at = lax.axis_index("tp")
    kv_head = tp_at * heads // QUERY_PER_KV
    scale = HEAD_SIZE ** (-0.5)
    q_tok, q_doc, q_pos = doc_pos(doc_lengths, ctx_at * token_length, token_length)
    cos_q, sin_q = rope_tables(q_pos)
    rot_q = apply_rotary(
        queries.reshape(token_length, heads, HEAD_SIZE).astype(jnp.float32), cos_q, sin_q
    ).astype(jnp.bfloat16)
    own_k = lax.dynamic_slice_in_dim(keys, kv_head * HEAD_SIZE, HEAD_SIZE, 1).astype(jnp.float32)
    rotated_keys = apply_rotary(own_k[:, None, :], cos_q, sin_q)[:, 0, :].astype(jnp.bfloat16)
    own_v = lax.dynamic_slice_in_dim(values, kv_head * HEAD_SIZE, HEAD_SIZE, 1)
    grads = grad_out.reshape(token_length, heads, HEAD_SIZE)
    gathered_k, gathered_v = (
        lax.all_gather(rotated_keys, "ctx", axis=0, tiled=True),
        lax.all_gather(own_v, "ctx", axis=0, tiled=True),
    )
    pieces = []
    for step in range(REACH + 1):
        source = (ctx_at - step) * token_length
        safe = jnp.maximum(source, 0)
        pieces.append(
            (
                lax.dynamic_slice_in_dim(gathered_k, safe, token_length, 0),
                lax.dynamic_slice_in_dim(gathered_v, safe, token_length, 0),
                source,
            )
        )
    state = (
        jnp.full((heads, token_length), NEG, jnp.float32),
        jnp.zeros((heads, token_length), jnp.float32),
        jnp.zeros((heads, token_length), jnp.float32),
    )
    saved = []
    for key_piece, value_piece, source in pieces:
        k_tok, k_doc, k_pos = doc_pos(doc_lengths, source, token_length)
        allowed = (q_doc[:, None] == k_doc[None, :]) & (k_tok[None, :] <= q_tok[:, None])

        def forward_live(current):
            top, total, weighted = current
            score = (
                jnp.einsum("qhd,kd->hqk", rot_q, key_piece, preferred_element_type=jnp.float32)
                * scale
            )
            score = jnp.where(allowed[None], score, NEG)
            dprod = jnp.einsum(
                "qhd,kd->hqk", grads, value_piece, preferred_element_type=jnp.float32
            )
            new_top = jnp.maximum(top, jnp.max(score, axis=2))
            decay = jnp.exp(top - new_top)
            expo = jnp.exp(score - new_top[..., None])
            return (
                (
                    new_top,
                    total * decay + jnp.sum(expo, axis=2),
                    weighted * decay + jnp.sum(expo * dprod, axis=2),
                ),
                score,
                dprod,
            )

        def forward_dead(current):
            empty = jnp.zeros((heads, token_length, token_length), jnp.float32)
            return (current, empty, empty)

        state, score, dprod = lax.cond(jnp.any(allowed), forward_live, forward_dead, state)
        saved.append((allowed, score, dprod))
    top, total, weighted = state
    lse = top + jnp.log(total)
    delta = weighted / total
    dq_acc = jnp.zeros((token_length, heads, HEAD_SIZE), jnp.float32)
    results = []
    for index in range(len(pieces)):
        allowed, score, dprod = saved[index]
        backward_key_piece = pieces[index][0]

        def backward_live(acc):
            prob = jnp.exp(score - lse[..., None])
            prob_b = prob.astype(jnp.bfloat16)
            dv_piece = jnp.einsum("hqk,qhd->kd", prob_b, grads, preferred_element_type=jnp.float32)
            dscore = (prob * (dprod - delta[..., None]) * scale).astype(jnp.bfloat16)
            acc = acc + jnp.einsum(
                "hqk,kd->qhd", dscore, backward_key_piece, preferred_element_type=jnp.float32
            )
            dk_piece = jnp.einsum("hqk,qhd->kd", dscore, rot_q, preferred_element_type=jnp.float32)
            return (acc, dk_piece, dv_piece)

        def backward_dead(acc):
            empty = jnp.zeros((token_length, HEAD_SIZE), jnp.float32)
            return (acc, empty, empty)

        dq_acc, run_dk_piece, run_dv_piece = lax.cond(
            jnp.any(allowed), backward_live, backward_dead, dq_acc
        )
        results.append((run_dk_piece, run_dv_piece))
    dq_acc, results = (dq_acc, results)
    dk_whole = jnp.zeros((n_ctx * token_length, HEAD_SIZE), jnp.float32)
    dv_whole = jnp.zeros((n_ctx * token_length, HEAD_SIZE), jnp.float32)
    for step in range(REACH + 1):
        safe = jnp.maximum((ctx_at - step) * token_length, 0)
        dk_piece, dv_piece = results[step]
        dk_whole = lax.dynamic_update_slice_in_dim(
            dk_whole, lax.dynamic_slice_in_dim(dk_whole, safe, token_length, 0) + dk_piece, safe, 0
        )
        dv_whole = lax.dynamic_update_slice_in_dim(
            dv_whole, lax.dynamic_slice_in_dim(dv_whole, safe, token_length, 0) + dv_piece, safe, 0
        )
    dk_own, dv_own = (
        lax.psum_scatter(dk_whole, "ctx", scatter_dimension=0, tiled=True),
        lax.psum_scatter(dv_whole, "ctx", scatter_dimension=0, tiled=True),
    )
    item_count = token_length // n_tp
    broad_zeros = jnp.zeros((token_length, KV_HEAD_COUNT * HEAD_SIZE), jnp.float32)
    dk_wide = lax.dynamic_update_slice_in_dim(broad_zeros, dk_own, kv_head * HEAD_SIZE, 1)
    dv_wide = lax.dynamic_update_slice_in_dim(broad_zeros, dv_own, kv_head * HEAD_SIZE, 1)
    key_grad_rows, dv_rows = (
        lax.psum_scatter(dk_wide, "tp", scatter_dimension=0, tiled=True),
        lax.psum_scatter(dv_wide, "tp", scatter_dimension=0, tiled=True),
    )
    r_tok, r_doc, r_pos = doc_pos(
        doc_lengths, ctx_at * token_length + tp_at * item_count, item_count
    )
    cosine_rows, sine_rows = rope_tables(r_pos)
    keys_gradient = (
        invert_rotary(
            key_grad_rows.reshape(item_count, KV_HEAD_COUNT, HEAD_SIZE), cosine_rows, sine_rows
        )
        .astype(jnp.bfloat16)
        .reshape(item_count, KV_HEAD_COUNT * HEAD_SIZE)
    )
    values_gradient = dv_rows.astype(jnp.bfloat16)
    grad_queries = (
        invert_rotary(dq_acc, cos_q, sin_q)
        .astype(jnp.bfloat16)
        .reshape(token_length, heads * HEAD_SIZE)
    )
    return (grad_queries, keys_gradient, values_gradient)


def solution(mesh):
    return jax.shard_map(
        local,
        mesh=mesh,
        in_specs=(P("ctx", "tp"), P("ctx", None), P("ctx", None), P("ctx", "tp"), P()),
        out_specs=(P("ctx", "tp"), P(("ctx", "tp"), None), P(("ctx", "tp"), None)),
        check_vma=False,
    )
```

profile of v0, /device:TPU:3, one launch (start us, length us, event | category | flops | bytes accessed | tf_op | source)
XLA Modules:
  0.0 290.2 jit_solution(8081659429790805632)
XLA Ops:
  8.9 1.5 copy.112
  10.4 1.6 convert.35
  12.9 11.4 %all-gather = bf16[2048,1,128]{0,2,1:T(8,128)(2,1)S(1)} all-gather(bf16[256,1,128]{0,2,1:T(8,128)(2,1)S(1)} %pad_maximum_fusion.2), channel_id=2, replica_groups=mesh['ctx'=8,'tp'=4] {'ctx'}, dimensions={0}, use_global_device_ids=true | all-gather | bytes 589824 | tf_op jit(solution)/shard_map/all_gather | solution.py:65
  25.5 8.9 %all_gather.7 = bf16[2048,128]{1,0:T(8,128)(2,1)S(1)} all-gather(bf16[256,128]{1,0:T(8,128)(2,1)S(1)} %constant_dynamic-slice_fusion.4), channel_id=1, replica_groups=mesh['ctx'=8,'tp'=4] {'ctx'}, dimensions={0}, use_global_device_ids=true | all-gather | bytes 589824 | tf_op jit(solution)/shard_map/all_gather | solution.py:66
  34.4 1.5 copy.113
  35.9 1.3 compare_and_fusion
  40.8 1.9 subtract_convert_fusion.1
  42.8 6.6 %conditional.10 = (f32[16,256]{1,0:T(8,128)}, f32[16,256]{1,0:T(8,128)S(1)}, f32[16,256]{1,0:T(8,128)S(1)}, f32[16,256,256]{1,2,0:T(8,128)}, f32[16,256,256]{1,2,0:T(8,128)S(1)}) conditional(s32[]{:T(128)} %convert_element_type.117, () %tuple.99, (pred[256,256]{0,1:T(8,128)(4,1)S(1)}, bf16[256,128]{1,0:T(8,128)(2,1)S(1)}, ...), branch_computations={%region_12.13_spmd, %region_13.17_spmd} | conditional | flops 544223232 | bytes 15056940 | solution.py:116
  42.8 2.7 fusion.80
  46.2 3.3 %multiply_reduce_fusion = (f32[16,256]{1,0:T(8,128)S(1)}, f32[16,256]{1,0:T(8,128)S(1)}, f32[16,256,256]{1,2,0:T(8,128)S(1)}) fusion(f32[16,256,256]{1,2,0:T(8,128)} %get-tuple-element.885, f32[16,256]{1,0:T(8,128)} %broadcast_maximum_fusion, bf16[256,16,128]{0,2,1:T(8,128)(2,1)S(1)} %get-tuple-element.717, bf16[2048,128]{1,0:T(8,128)(2,1)S(1)} %get-tuple-element.287, ...), kind=kOutput, calls=%fused_computation.1 | convolution fusion | flops 272621568 | bytes 9551876 | tf_op jit(solution)/shard_map/cond/branch_1_fun/qhd,kd->hqk/dot_general | solution.py:96
  49.5 1.9 copy-done.2
  51.4 8.1 %conditional.11 = (f32[16,256]{1,0:T(8,128)}, f32[16,256]{1,0:T(8,128)S(1)}, f32[16,256]{1,0:T(8,128)S(1)}, f32[16,256,256]{1,2,0:T(8,128)}, f32[16,256,256]{1,2,0:T(8,128)S(1)}) conditional(s32[]{:T(128)} %convert_element_type.116, (f32[16,256]{1,0:T(8,128)}, f32[16,256]{1,0:T(8,128)S(1)}, f32[16,256]{1,0:T(8,128)S(1)}) %tuple.101, ...), branch_computations={%region_17.18_spmd, %region_18.22_spmd} | conditional | flops 544223232 | bytes 15155244 | solution.py:116
  51.4 2.7 fusion.81
  54.8 3.3 %multiply_reduce_fusion.1 = (f32[16,256]{1,0:T(8,128)S(1)}, f32[16,256]{1,0:T(8,128)S(1)}, f32[16,256,256]{1,2,0:T(8,128)S(1)}) fusion(f32[16,256,256]{1,2,0:T(8,128)} %get-tuple-element.895, f32[16,256]{1,0:T(8,128)S(1)} %max.11, bf16[256,16,128]{0,2,1:T(8,128)(2,1)S(1)} %get-tuple-element.726, bf16[2048,128]{1,0:T(8,128)(2,1)S(1)} %get-tuple-element.299, ...), kind=kOutput, calls=%fused_computation.14 | convolution fusion | flops 272621568 | bytes 9551876 | tf_op jit(solution)/shard_map/cond/branch_1_fun/qhd,kd->hqk/dot_general | solution.py:96
  59.5 2.0 copy-done.3
  61.4 8.0 %conditional.12 = (f32[16,256]{1,0:T(8,128)}, f32[16,256]{1,0:T(8,128)S(1)}, f32[16,256]{1,0:T(8,128)S(1)}, f32[16,256,256]{1,2,0:T(8,128)}, f32[16,256,256]{1,2,0:T(8,128)S(1)}) conditional(s32[]{:T(128)} %convert_element_type.114, (f32[16,256]{1,0:T(8,128)}, f32[16,256]{1,0:T(8,128)S(1)}, f32[16,256]{1,0:T(8,128)S(1)}) %tuple.103, ...), branch_computations={%region_22.23_spmd, %region_23.27_spmd} | conditional | flops 544223232 | bytes 15155244 | solution.py:116
  61.4 2.7 fusion.82
  64.8 3.3 %multiply_reduce_fusion.2 = (f32[16,256]{1,0:T(8,128)S(1)}, f32[16,256]{1,0:T(8,128)S(1)}, f32[16,256,256]{1,2,0:T(8,128)S(1)}) fusion(f32[16,256,256]{1,2,0:T(8,128)} %get-tuple-element.905, f32[16,256]{1,0:T(8,128)S(1)} %max.28, bf16[256,16,128]{0,2,1:T(8,128)(2,1)S(1)} %get-tuple-element.735, bf16[2048,128]{1,0:T(8,128)(2,1)S(1)} %get-tuple-element.311, ...), kind=kOutput, calls=%fused_computation.26 | convolution fusion | flops 272621568 | bytes 9551876 | tf_op jit(solution)/shard_map/cond/branch_1_fun/qhd,kd->hqk/dot_general | solution.py:96
  69.5 2.0 copy-done.4
  71.4 3.1 %conditional.13 = (f32[16,256]{1,0:T(8,128)}, f32[16,256]{1,0:T(8,128)S(1)}, f32[16,256]{1,0:T(8,128)S(1)}, f32[16,256,256]{1,2,0:T(8,128)}, f32[16,256,256]{1,2,0:T(8,128)S(1)}) conditional(s32[]{:T(128)} %convert_element_type.112, (f32[16,256]{1,0:T(8,128)}, f32[16,256]{1,0:T(8,128)S(1)}, f32[16,256]{1,0:T(8,128)S(1)}) %tuple.105, ...), branch_computations={%region_27.28_spmd, %region_28.32_spmd} | conditional | flops 544223232 | bytes 15155244 | solution.py:116
  71.4 2.5 broadcast.298
  74.5 2.0 copy-done.5
  76.5 2.8 conditional.14
  76.5 2.4 broadcast.300
  80.0 1.2 copy-done.6
  81.2 10.3 %conditional.15 = (f32[256,16,128]{2,0,1:T(8,128)}, f32[256,128]{1,0:T(8,128)S(1)}, f32[256,128]{1,0:T(8,128)S(1)}) conditional(s32[]{:T(128)} %convert_element_type.117, () %tuple.98, (f32[16,256]{1,0:T(8,128)S(1)}, f32[16,256,256]{1,2,0:T(8,128)}, f32[16,256]{1,0:T(8,128)S(1)}, f32[16,256,256]{1,2,0:T(8,128)}, bf16[256,128]{1,0:T(8,128)(2,1)S(1)}, ...), branch_computations={%region_37.38_spmd, %region_38.39_spmd} | conditional | flops 812646400 | bytes 23445528 | solution.py:142
  81.2 4.5 %multiply_convert_fusion = bf16[16,256,256]{1,2,0:T(8,128)(2,1)S(1)} fusion(f32[16,256,256]{1,2,0:T(8,128)} %get-tuple-element.340, f32[16,256,256]{1,2,0:T(8,128)} %get-tuple-element.338, f32[16,256]{1,0:T(8,128)S(1)} %get-tuple-element.341, f32[16,256]{1,0:T(8,128)S(1)} %get-tuple-element.339), kind=kLoop, calls=%fused_computation.61 | loop fusion | flops 5242880 | bytes 10518528 | tf_op jit(solution)/shard_map/cond/branch_1_fun/convert_element_type | solution.py:131
  85.7 2.1 convolution_bitcast_fusion.5
  88.6 2.9 fusion.31
  91.5 11.9 %conditional.16 = (f32[256,16,128]{2,0,1:T(8,128)}, f32[256,128]{1,0:T(8,128)S(1)}, f32[256,128]{1,0:T(8,128)S(1)}) conditional(s32[]{:T(128)} %convert_element_type.116, f32[256,16,128]{2,0,1:T(8,128)} %get-tuple-element.437, (f32[16,256]{1,0:T(8,128)S(1)}, f32[16,256,256]{1,2,0:T(8,128)}, f32[16,256]{1,0:T(8,128)S(1)}, ...), branch_computations={%region_39.40_spmd, %region_40.41_spmd} | conditional | flops 813170688 | bytes 25542680 | solution.py:142
  91.5 4.5 %multiply_convert_fusion.1 = bf16[16,256,256]{1,2,0:T(8,128)(2,1)S(1)} fusion(f32[16,256,256]{1,2,0:T(8,128)} %get-tuple-element.348, f32[16,256,256]{1,2,0:T(8,128)} %get-tuple-element.346, f32[16,256]{1,0:T(8,128)S(1)} %get-tuple-element.349, f32[16,256]{1,0:T(8,128)S(1)} %get-tuple-element.347), kind=kLoop, calls=%fused_computation.70 | loop fusion | flops 5242880 | bytes 10518528 | tf_op jit(solution)/shard_map/cond/branch_1_fun/convert_element_type | solution.py:131
  96.0 3.7 %bitcast_add_fusion = f32[256,16,128]{2,0,1:T(8,128)} fusion(f32[256,16,128]{2,0,1:T(8,128)} %get-tuple-element.345, bf16[16,256,256]{1,2,0:T(8,128)(2,1)S(1)} %multiply_convert_fusion.1, bf16[256,128]{1,0:T(8,128)(2,1)S(1)} %get-tuple-element.350), kind=kOutput, calls=%fused_computation.74 | convolution fusion | flops 268959744 | bytes 6356992 | tf_op jit(solution)/shard_map/cond/branch_1_fun/hqk,kd->qhd/dot_general | solution.py:132
  100.5 2.9 fusion.39
  104.1 11.9 %conditional.17 = (f32[256,16,128]{2,0,1:T(8,128)}, f32[256,128]{1,0:T(8,128)S(1)}, f32[256,128]{1,0:T(8,128)S(1)}) conditional(s32[]{:T(128)} %convert_element_type.114, f32[256,16,128]{2,0,1:T(8,128)} %get-tuple-element.440, (f32[16,256]{1,0:T(8,128)S(1)}, f32[16,256,256]{1,2,0:T(8,128)}, f32[16,256]{1,0:T(8,128)S(1)}, ...), branch_computations={%region_41.42_spmd, %region_42.43_spmd} | conditional | flops 813170688 | bytes 25542680 | solution.py:142
  104.1 4.5 %multiply_convert_fusion.2 = bf16[16,256,256]{1,2,0:T(8,128)(2,1)S(1)} fusion(f32[16,256,256]{1,2,0:T(8,128)} %get-tuple-element.356, f32[16,256,256]{1,2,0:T(8,128)} %get-tuple-element.354, f32[16,256]{1,0:T(8,128)S(1)} %get-tuple-element.357, f32[16,256]{1,0:T(8,128)S(1)} %get-tuple-element.355), kind=kLoop, calls=%fused_computation.79 | loop fusion | flops 5242880 | bytes 10518528 | tf_op jit(solution)/shard_map/cond/branch_1_fun/convert_element_type | solution.py:131
  108.6 3.7 %bitcast_add_fusion.1 = f32[256,16,128]{2,0,1:T(8,128)} fusion(f32[256,16,128]{2,0,1:T(8,128)} %get-tuple-element.353, bf16[16,256,256]{1,2,0:T(8,128)(2,1)S(1)} %multiply_convert_fusion.2, bf16[256,128]{1,0:T(8,128)(2,1)S(1)} %get-tuple-element.358), kind=kOutput, calls=%fused_computation.83 | convolution fusion | flops 268959744 | bytes 6356992 | tf_op jit(solution)/shard_map/cond/branch_1_fun/hqk,kd->qhd/dot_general | solution.py:132
  113.1 2.9 fusion.47
  120.8 1.0 dynamic_update_slice.37
  122.8 1.0 dynamic_update_slice.38
  126.7 1.0 dynamic_update_slice.40
  135.1 63.3 %reduce-scatter.5.cloned.1.call-done = f32[256,128]{1,0:T(8,128)} async-done(((f32[2048,128]{1,0:T(8,128)}), f32[256,128]{1,0:T(8,128)}) %reduce-scatter.5.cloned.1.call-update) | async-done | bytes 131088 | tf_op jit(solution)/shard_map/reduce_scatter | solution.py:159
  200.3 2.9 %copy.138 = f32[256,16,128]{0,2,1:T(8,128)} copy(f32[256,16,128]{2,0,1:T(8,128)} %get-tuple-element.449) | data formatting | bytes 4194304 | tf_op jit(solution)/shard_map/cond | solution.py:142
  203.2 1.9 add_convert_fusion
  205.2 1.4 copy.140
  206.7 30.9 %reduce-scatter.9.cloned.1.call-done = f32[256,128]{1,0:T(8,128)} async-done(((f32[2048,128]{1,0:T(8,128)}), f32[256,128]{1,0:T(8,128)}) %reduce-scatter.9.cloned.1.call-update) | async-done | bytes 131088 | tf_op jit(solution)/shard_map/reduce_scatter | solution.py:160
  239.7 20.3 %reduce-scatter.7.cloned.1.call-done = f32[64,512]{1,0:T(8,128)} async-done(((f32[256,512]{1,0:T(8,128)}), f32[64,512]{1,0:T(8,128)}) %reduce-scatter.7.cloned.1.call-update) | async-done | bytes 131088 | tf_op jit(solution)/shard_map/reduce_scatter | solution.py:167
  261.9 20.2 %reduce-scatter.11.cloned.1.call-done = f32[64,512]{1,0:T(8,128)} async-done(((f32[256,512]{1,0:T(8,128)}), f32[64,512]{1,0:T(8,128)}) %reduce-scatter.11.cloned.1.call-update) | async-done | bytes 131088 | tf_op jit(solution)/shard_map/reduce_scatter | solution.py:168
  282.1 1.5 convert_element_type.126
  (129 shorter events, 35.1 us)
Async XLA Ops:
  7.2 4.8 %copy-start = (bf16[256,512]{1,0:T(8,128)(2,1)S(1)}, bf16[256,512]{1,0:T(8,128)(2,1)}, u32[]{:S(2)}) copy-start(bf16[256,512]{1,0:T(8,128)(2,1)} %param.26) | copy-start | bytes 786436
  7.2 191.3 %reduce-scatter.5.cloned.1.call-start = ((), (), s32[]{:S(2)}) async-start(), calls=%async_computation.4 | async-start | bytes 1179648 | tf_op jit(solution)/shard_map/reduce_scatter | solution.py:159
  49.5 1.9 copy-start.2
  59.5 2.0 copy-start.3
  69.5 2.0 copy-start.4
  74.5 2.0 copy-start.5
  79.3 1.9 copy-start.6
  103.4 0.7 copy-start.11
  103.4 0.7 copy-start.12
  116.0 0.6 copy-start.14
  116.0 0.7 copy-start.15
  116.7 0.7 copy-start.17
  116.7 0.7 copy-start.18
  117.5 0.7 copy-start.20
  118.1 0.6 copy-start.21
  118.8 11.1 %copy-start.13 = (f32[256,128]{1,0:T(8,128)S(1)}, f32[256,128]{1,0:T(8,128)}, u32[]{:S(2)}) copy-start(f32[256,128]{1,0:T(8,128)} %copy-done.12) | copy-start | bytes 393220
  118.8 12.1 %copy-start.16 = (f32[256,128]{1,0:T(8,128)S(1)}, f32[256,128]{1,0:T(8,128)}, u32[]{:S(2)}) copy-start(f32[256,128]{1,0:T(8,128)} %copy-done.15) | copy-start | bytes 393220
  118.8 13.2 %copy-start.19 = (f32[256,128]{1,0:T(8,128)S(1)}, f32[256,128]{1,0:T(8,128)}, u32[]{:S(2)}) copy-start(f32[256,128]{1,0:T(8,128)} %copy-done.18) | copy-start | bytes 393220
  118.8 14.2 %copy-start.22 = (f32[256,128]{1,0:T(8,128)S(1)}, f32[256,128]{1,0:T(8,128)}, u32[]{:S(2)}) copy-start(f32[256,128]{1,0:T(8,128)} %copy-done.21) | copy-start | bytes 393220
  127.7 1.0 copy-start.8
  128.7 109.0 %reduce-scatter.9.cloned.1.call-start = ((), (), s32[]{:S(2)}) async-start(), calls=%async_computation.6 | async-start | bytes 1179648 | tf_op jit(solution)/shard_map/reduce_scatter | solution.py:160
  134.1 1.0 copy-start.7
  135.1 125.0 %reduce-scatter.7.cloned.1.call-start = ((), (), s32[]{:S(2)}) async-start(), calls=%async_computation.5 | async-start | bytes 655360 | tf_op jit(solution)/shard_map/reduce_scatter | solution.py:167
  199.4 0.8 copy-start.10
  200.2 81.9 %reduce-scatter.11.cloned.1.call-start = ((), (), s32[]{:S(2)}) async-start(), calls=%async_computation.7 | async-start | bytes 655360 | tf_op jit(solution)/shard_map/reduce_scatter | solution.py:168
  203.2 80.4 %copy-start.1 = (bf16[256,512]{1,0:T(8,128)(2,1)S(1)}, bf16[256,512]{1,0:T(8,128)(2,1)}, u32[]{:S(2)}) copy-start(bf16[256,512]{1,0:T(8,128)(2,1)} %param.26) | copy-start | bytes 786436
  238.6 0.8 copy-start.9
Sparse Core Ops, SparseCore 0:
  128.8 69.5 reduce-scatter.4
  201.6 35.9 reduce-scatter.8
  239.9 20.0 reduce-scatter.6
  262.2 19.9 reduce-scatter.10
where the time goes:
time: 295 us; the launch traced here: 290 us
  waiting for transfers between devices  135 us (46%)
  local copies, waits for them, and re-layouts  45.6 us (15%)
  matrix products  38.3 us (13%)
  other arithmetic  33.1 us (11%)
  blocking collectives  20.3 us (7%)
  between operations  17.7 us (6%)
    reduce_scatter x1, waiting for transfers between devices, local(): lax.psum_scatter(dk_whole, 'ctx', scatter_dimension=0, tiled=True)  63.3 us
    reduce_scatter x1, waiting for transfers between devices, local(): lax.psum_scatter(dv_whole, 'ctx', scatter_dimension=0, tiled=True)  30.9 us
    unnamed x51, local copies, waits for them, and re-layouts  21 us
    reduce_scatter x1, waiting for transfers between devices, local(): lax.psum_scatter(dk_wide, 'tp', scatter_dimension=0, tiled=True)  20.3 us
    reduce_scatter x1, waiting for transfers between devices, local(): lax.psum_scatter(dv_wide, 'tp', scatter_dimension=0, tiled=True)  20.2 us
    convert_element_type x3, other arithmetic, backward_live(): dscore = (prob * (dprod - delta[..., None]) * scale).astype(jnp.bfloat16)  13.6 us
    all_gather x1, blocking collectives, local(): lax.all_gather(rotated_keys, 'ctx', axis=0, tiled=True)  11.4 us
    dot_general x3, matrix products, forward_live(): jnp.einsum('qhd,kd->hqk', grads, value_piece, preferred_element_type=jnp....  9.83 us
  transfers between devices with their start and end apart: 4, of which 4 were waited for; matrix products, arithmetic and copies ran while one was open for 5% of the time, Pallas kernels for 0%

commit v1 on v0

v1 whole, which is shorter than its diff:
```python
import functools
import math

import jax
import jax.numpy as jnp
from jax import lax
from jax.experimental import pallas as pl
from jax.experimental.pallas import tpu as pltpu
from jax.sharding import PartitionSpec as P

KV_HEAD_COUNT = 4
HEAD_SIZE = 128
QUERY_PER_KV = 16
MAXDOC = 1024
NEG = -1e30
HALF = HEAD_SIZE // 2
SCALE = HEAD_SIZE ** (-0.5)
LOG2E = math.log2(math.e)
HEADS_PER_STEP = 2
VMEM_LIMIT = 48 << 20
MESH = pl.DeviceIdType.MESH


def doc_pos(doc_lengths, first, item_count):
    starts = jnp.cumsum(doc_lengths) - doc_lengths
    tok = first + jnp.arange(item_count, dtype=jnp.int32)
    start_of = jnp.max(jnp.where(starts[None, :] <= tok[:, None], starts[None, :], 0), axis=1)
    return tok, start_of, tok - start_of


def rope_tables(pos):
    freq = 500000.0 ** (-(2.0 * jnp.arange(HALF, dtype=jnp.float32)) / HEAD_SIZE)
    angle = pos.astype(jnp.float32)[:, None] * freq[None, :]
    return jnp.cos(angle), jnp.sin(angle)


def greet(peers):
    barrier = pltpu.get_barrier_semaphore()
    count = 0
    for live, device in peers:
        @pl.when(live)
        def _():
            pl.semaphore_signal(barrier, inc=1, device_id=device, device_id_type=MESH)
        count = count + live.astype(jnp.int32)
    pl.semaphore_wait(barrier, count)


def gather_kernel(n_ctx, reach, own_ref, win_ref, send_sem, recv_sem, local_sem):
    rows = own_ref.shape[1]
    me = lax.axis_index("ctx")
    at = lax.axis_index("tp")
    greet(
        [(me + s < n_ctx, (lax.rem(me + s, n_ctx), at)) for s in range(1, reach + 1)]
        + [(me - s >= 0, (lax.rem(me - s + n_ctx, n_ctx), at)) for s in range(1, reach + 1)]
    )

    def copy(s):
        return pltpu.make_async_remote_copy(
            src_ref=own_ref,
            dst_ref=win_ref.at[:, pl.ds((reach - s) * rows, rows), :],
            send_sem=send_sem.at[s - 1],
            recv_sem=recv_sem.at[s - 1],
            device_id=(lax.rem(me + s, n_ctx), at),
            device_id_type=MESH,
        )

    for s in range(reach, 0, -1):
        @pl.when(me + s < n_ctx)
        def _():
            copy(s).start()
    mine = pltpu.make_async_copy(own_ref, win_ref.at[:, pl.ds(reach * rows, rows), :], local_sem)
    mine.start()
    mine.wait()
    for s in range(1, reach + 1):
        @pl.when(me - s >= 0)
        def _():
            copy(s).wait_recv()
    for s in range(1, reach + 1):
        @pl.when(me + s < n_ctx)
        def _():
            copy(s).wait_send()


def gather(own, n_ctx, reach):
    two, rows, width = own.shape
    return pl.pallas_call(
        functools.partial(gather_kernel, n_ctx, reach),
        out_shape=jax.ShapeDtypeStruct((two, (reach + 1) * rows, width), own.dtype),
        in_specs=[pl.BlockSpec(memory_space=pl.ANY)],
        out_specs=pl.BlockSpec(memory_space=pl.ANY),
        scratch_shapes=[
            pltpu.SemaphoreType.DMA((reach,)),
            pltpu.SemaphoreType.DMA((reach,)),
            pltpu.SemaphoreType.DMA,
        ],
        compiler_params=pltpu.CompilerParams(collective_id=0, has_side_effects=True),
        name="gather_kv",
    )(own)


def attend_kernel(
    reach, rows, low_ref, win_ref, q_ref, g_ref, cos_ref, sin_ref, cos_t_ref, sin_t_ref, start_ref,
    dq_ref, far_ref, own_ref, bias, kt, dk, dv,
):
    step = pl.program_id(0)
    span = (reach + 1) * rows

    @pl.when(step == 0)
    def _():
        key = lax.broadcasted_iota(jnp.int32, (span, rows), 0)
        query = lax.broadcasted_iota(jnp.int32, (span, rows), 1) + reach * rows
        allowed = (key >= start_ref[...]) & (key <= query)
        bias[...] = jnp.where(allowed, 0.0, NEG)
        kt[...] = win_ref[0].T
        dk[...] = jnp.zeros_like(dk)
        dv[...] = jnp.zeros_like(dv)

    nt = (((1,), (1,)), ((), ()))

    def work(tiles):
        base = span - tiles * rows
        keys = win_ref[0, base:, :]
        values = win_ref[1, base:, :]
        probs, grads, dscores, queries = [], [], [], []
        for i in range(HEADS_PER_STEP):
            cols = slice(i * HEAD_SIZE, (i + 1) * HEAD_SIZE)
            raw = q_ref[:, cols].astype(jnp.float32)
            rot = raw * cos_ref[...] + pltpu.roll(raw, HALF, 1) * sin_ref[...]
            rot = rot.astype(jnp.bfloat16)
            grad = g_ref[:, cols]
            score = lax.dot_general(keys, rot, nt, preferred_element_type=jnp.float32)
            score = score * (SCALE * LOG2E) + bias[base:, :]
            top = jnp.max(score, axis=0, keepdims=True)
            expo = jnp.exp2(score - top)
            total = jnp.sum(expo, axis=0, keepdims=True)
            dprod = lax.dot_general(values, grad, nt, preferred_element_type=jnp.float32)
            weighted = jnp.sum(expo * dprod, axis=0, keepdims=True)
            inv = 1.0 / total
            delta = weighted * inv
            probs.append(expo.astype(jnp.bfloat16))
            dscore = (expo * (dprod - delta)).astype(jnp.bfloat16)
            dscores.append(dscore)
            spread = jnp.broadcast_to(inv, (HEAD_SIZE, rows)).T
            grads.append((grad.astype(jnp.float32) * spread).astype(jnp.bfloat16))
            queries.append((rot.astype(jnp.float32) * (spread * SCALE)).astype(jnp.bfloat16))
            dq = jnp.dot(kt[:, base:], dscore, preferred_element_type=jnp.float32)
            dq = dq * (inv * SCALE)
            one, two = dq[:HALF], dq[HALF:]
            c, s = cos_t_ref[...], sin_t_ref[...]
            turned = jnp.concatenate([one * c + two * s, two * c - one * s], axis=0)
            dq_ref[:, cols] = turned.T.astype(jnp.bfloat16)
        dv[base:, :] += jnp.dot(
            jnp.concatenate(probs, axis=1), jnp.concatenate(grads, axis=0),
            preferred_element_type=jnp.float32,
        )
        dk[base:, :] += jnp.dot(
            jnp.concatenate(dscores, axis=1), jnp.concatenate(queries, axis=0),
            preferred_element_type=jnp.float32,
        )

    tiles = reach + 1 - low_ref[0] // rows
    for count in range(1, reach + 2):
        @pl.when(tiles == count)
        def _():
            work(count)

    @pl.when(step == pl.num_programs(0) - 1)
    def _():
        far_ref[0] = dk[: reach * rows, :].astype(jnp.bfloat16)
        far_ref[1] = dv[: reach * rows, :].astype(jnp.bfloat16)
        own_ref[0] = dk[reach * rows :, :]
        own_ref[1] = dv[reach * rows :, :]


def attend(window, queries, grad_out, low, start_row, cos, sin, reach):
    rows, width = queries.shape
    span = (reach + 1) * rows
    block = HEADS_PER_STEP * HEAD_SIZE
    steps = width // block
    cos_wide = jnp.concatenate([cos, cos], axis=1)
    sin_wide = jnp.concatenate([-sin, sin], axis=1)

    def whole(shape):
        return pl.BlockSpec(shape, lambda i, low: (0,) * len(shape))

    by_head = pl.BlockSpec((rows, block), lambda i, low: (0, i))
    return pl.pallas_call(
        functools.partial(attend_kernel, reach, rows),
        grid_spec=pltpu.PrefetchScalarGridSpec(
            num_scalar_prefetch=1,
            grid=(steps,),
            in_specs=[
                whole((2, span, HEAD_SIZE)), by_head, by_head,
                whole((rows, HEAD_SIZE)), whole((rows, HEAD_SIZE)),
                whole((HALF, rows)), whole((HALF, rows)), whole((1, rows)),
            ],
            out_specs=[
                by_head, whole((2, reach * rows, HEAD_SIZE)), whole((2, rows, HEAD_SIZE)),
            ],
            scratch_shapes=[
                pltpu.VMEM((span, rows), jnp.float32),
                pltpu.VMEM((HEAD_SIZE, span), jnp.bfloat16),
                pltpu.VMEM((span, HEAD_SIZE), jnp.float32),
                pltpu.VMEM((span, HEAD_SIZE), jnp.float32),
            ],
        ),
        out_shape=[
            jax.ShapeDtypeStruct((rows, width), jnp.bfloat16),
            jax.ShapeDtypeStruct((2, reach * rows, HEAD_SIZE), jnp.bfloat16),
            jax.ShapeDtypeStruct((2, rows, HEAD_SIZE), jnp.float32),
        ],
        compiler_params=pltpu.CompilerParams(
            dimension_semantics=("arbitrary",), vmem_limit_bytes=VMEM_LIMIT
        ),
        name="attend",
    )(low, window, queries, grad_out, cos_wide, sin_wide, cos.T, sin.T, start_row)


def scatter_kernel(
    n_ctx, n_tp, reach, share, far_ref, own_ref, cos_ref, sin_ref, key_out, value_out,
    acc, landed, staged, pieces, send_sem, recv_sem, piece_send, piece_recv,
):
    rows = own_ref.shape[1]
    items = rows // n_tp
    me = lax.axis_index("ctx")
    at = lax.axis_index("tp")
    greet(
        [(me - s >= 0, (lax.rem(me - s + n_ctx, n_ctx), at)) for s in range(1, reach + 1)]
        + [(me + s < n_ctx, (lax.rem(me + s, n_ctx), at)) for s in range(1, reach + 1)]
        + [(at >= 0, (me, lax.rem(at + t, n_tp))) for t in range(1, n_tp)]
    )

    def copy(s):
        return pltpu.make_async_remote_copy(
            src_ref=far_ref.at[:, pl.ds((reach - s) * rows, rows), :],
            dst_ref=landed.at[s - 1],
            send_sem=send_sem.at[s - 1],
            recv_sem=recv_sem.at[s - 1],
            device_id=(lax.rem(me - s + n_ctx, n_ctx), at),
            device_id_type=MESH,
        )

    for s in range(reach, 0, -1):
        @pl.when(me - s >= 0)
        def _():
            copy(s).start()
    acc[...] = own_ref[...]
    for s in range(1, reach + 1):
        @pl.when(me + s < n_ctx)
        def _():
            copy(s).wait_recv()
            acc[...] += landed[s - 1].astype(jnp.float32)
    grad = acc[0]
    turned = grad * cos_ref[...] - pltpu.roll(grad, HALF, 1) * sin_ref[...]
    staged[0] = turned.astype(staged.dtype)
    staged[1] = acc[1].astype(staged.dtype)

    def piece(t):
        to = lax.rem(at + t, n_tp)
        return pltpu.make_async_remote_copy(
            src_ref=staged.at[:, pl.ds(pl.multiple_of(to * items, items), items), :],
            dst_ref=pieces.at[t],
            send_sem=piece_send.at[t - 1],
            recv_sem=piece_recv.at[t - 1],
            device_id=(me, to),
            device_id_type=MESH,
        )

    for t in range(1, n_tp):
        piece(t).start()
    pieces[0] = staged[:, pl.ds(pl.multiple_of(at * items, items), items), :]
    for t in range(1, n_tp):
        piece(t).wait_recv()
    for head in range(KV_HEAD_COUNT):
        cols = slice(head * HEAD_SIZE, (head + 1) * HEAD_SIZE)
        total = None
        for other in range(head * share, (head + 1) * share):
            got = pieces[lax.rem(at - other + n_tp, n_tp)]
            total = got if total is None else total + got
        key_out[:, cols] = total[0].astype(jnp.bfloat16)
        value_out[:, cols] = total[1].astype(jnp.bfloat16)
    for t in range(1, n_tp):
        piece(t).wait_send()
    for s in range(1, reach + 1):
        @pl.when(me - s >= 0)
        def _():
            copy(s).wait_send()


def scatter(far, own, cos_wide, sin_wide, n_ctx, n_tp, reach, share):
    rows = own.shape[1]
    items = rows // n_tp
    between = jnp.bfloat16 if share == 1 else jnp.float32
    vmem = pl.BlockSpec(memory_space=pltpu.VMEM)
    width = KV_HEAD_COUNT * HEAD_SIZE
    return pl.pallas_call(
        functools.partial(scatter_kernel, n_ctx, n_tp, reach, share),
        out_shape=[jax.ShapeDtypeStruct((items, width), jnp.bfloat16)] * 2,
        in_specs=[vmem] * 4,
        out_specs=[vmem] * 2,
        scratch_shapes=[
            pltpu.VMEM((2, rows, HEAD_SIZE), jnp.float32),
            pltpu.VMEM((reach, 2, rows, HEAD_SIZE), jnp.bfloat16),
            pltpu.VMEM((2, rows, HEAD_SIZE), between),
            pltpu.VMEM((n_tp, 2, items, HEAD_SIZE), between),
            pltpu.SemaphoreType.DMA((reach,)),
            pltpu.SemaphoreType.DMA((reach,)),
            pltpu.SemaphoreType.DMA((n_tp - 1,)),
            pltpu.SemaphoreType.DMA((n_tp - 1,)),
        ],
        compiler_params=pltpu.CompilerParams(
            collective_id=1, has_side_effects=True, vmem_limit_bytes=VMEM_LIMIT
        ),
        name="scatter_grads",
    )(far, own, cos_wide, sin_wide)


def local(queries, keys, values, grad_out, doc_lengths):
    rows = queries.shape[0]
    heads = queries.shape[1] // HEAD_SIZE
    n_ctx = lax.axis_size("ctx")
    n_tp = lax.axis_size("tp")
    at = lax.axis_index("tp")
    head = at * heads // QUERY_PER_KV
    share = max(1, QUERY_PER_KV // heads)
    reach = min(-(-MAXDOC // rows), n_ctx - 1)
    first = lax.axis_index("ctx") * rows
    tok, start_of, pos = doc_pos(doc_lengths, first, rows)
    cos, sin = rope_tables(pos)
    start_row = (start_of - (first - reach * rows))[None, :]
    low = start_row[0, :1]
    key = lax.dynamic_slice_in_dim(keys, head * HEAD_SIZE, HEAD_SIZE, 1).astype(jnp.float32)
    value = lax.dynamic_slice_in_dim(values, head * HEAD_SIZE, HEAD_SIZE, 1)
    one, two = key[:, :HALF], key[:, HALF:]
    key = jnp.concatenate([one * cos - two * sin, two * cos + one * sin], axis=1)
    own = jnp.stack([key.astype(jnp.bfloat16), value])
    window = gather(own, n_ctx, reach)
    grad_queries, far, near = attend(window, queries, grad_out, low, start_row, cos, sin, reach)
    cos_wide = jnp.concatenate([cos, cos], axis=1)
    sin_wide = jnp.concatenate([-sin, sin], axis=1)
    keys_gradient, values_gradient = scatter(
        far, near, cos_wide, sin_wide, n_ctx, n_tp, reach, share
    )
    return grad_queries, keys_gradient, values_gradient


def solution(mesh):
    return jax.shard_map(
        local,
        mesh=mesh,
        in_specs=(P("ctx", "tp"), P("ctx", None), P("ctx", None), P("ctx", "tp"), P()),
        out_specs=(P("ctx", "tp"), P(("ctx", "tp"), None), P(("ctx", "tp"), None)),
        check_vma=False,
    )
```

time: 295 us -> 55.2 us (0.19); the launches traced: 290 us -> 54.6 us
  waiting for transfers between devices: 135 us -> 0 us
  Pallas kernels: 0 us -> 47.4 us
  local copies, waits for them, and re-layouts: 45.6 us -> 3.56 us
  matrix products: 38.3 us -> 0 us
  other arithmetic: 33.1 us -> 2.92 us
  blocking collectives: 20.3 us -> 0 us
  between operations: 17.7 us -> 0.76 us
    reduce_scatter x4 -> x0, waiting for transfers between devices: 135 us -> none  [the longest x1 63.3 us: local(): lax.psum_scatter(dk_whole, 'ctx', scatter_dimension=0, tiled=True)]
    pallas_call x0 -> x3, Pallas kernels: none -> 47.4 us  [the longest x1 25.1 us: scatter(): pl.pallas_call(functools.partial(scatter_kernel, n_ctx, n_tp, reach, shar...]
    dot_general x15 -> x0, matrix products: 38.3 us -> none  [the longest x3 9.83 us: forward_live(): jnp.einsum('qhd,kd->hqk', grads, value_piece, preferred_element_type=jnp....]
    all_gather x2 -> x0, blocking collectives: 20.3 us -> none  [the longest x1 11.4 us: local(): lax.all_gather(rotated_keys, 'ctx', axis=0, tiled=True)]
    unnamed x51 -> x12, local copies, waits for them, and re-layouts: 21 us -> 3.03 us
    convert_element_type x5 -> x1, other arithmetic: 16.7 us -> 0.86 us  [local(): lax.dynamic_slice_in_dim(keys, head * HEAD_SIZE, HEAD_SIZE, 1)]
    dynamic_update_slice x12 -> x0, local copies, waits for them, and re-layouts: 11.9 us -> none  [the longest x5 5.05 us: local(): lax.dynamic_update_slice_in_dim(dv_whole, lax.dynamic_slice_in_dim(dv_who...]
    another operation x10 -> x1, local copies, waits for them, and re-layouts: 5.83 us -> 0.01 us  [local(): own = jnp.stack([key.astype(jnp.bfloat16), value])]
  transfers between devices with their start and end apart: 4 -> 0, of which waited for: 4 -> 0; matrix products, arithmetic and copies ran while one was open for 5% -> 0% of each run, Pallas kernels for 0% -> 0%
where the time goes in v1:
time: 55.2 us; the launch traced here: 54.6 us
  Pallas kernels  47.4 us (86%)
  local copies, waits for them, and re-layouts  3.56 us (6%)
  other arithmetic  2.92 us (5%)
  between operations  0.76 us (1%)
    pallas_call x1, Pallas kernels, scatter(): pl.pallas_call(functools.partial(scatter_kernel, n_ctx, n_tp, reach, shar...  25.1 us
    pallas_call x1, Pallas kernels, attend(): pl.pallas_call(functools.partial(attend_kernel, reach, rows), grid_spec=p...  14.4 us
    pallas_call x1, Pallas kernels, gather(): pl.pallas_call(functools.partial(gather_kernel, n_ctx, reach), out_shape=...  7.93 us
    unnamed x12, local copies, waits for them, and re-layouts  3.03 us

profile of v1, /device:TPU:3, one launch (start us, length us, event | category | flops | bytes accessed | tf_op | source)
XLA Modules:
  0.0 54.6 jit_solution(1343343968740532517)
XLA Ops:
  0.6 0.0 copy-start
  0.7 0.0 copy-start.4
  0.7 0.7 %copy-done.4 = s32[4]{0:T(128)S(1)} copy-done((s32[4]{0:T(128)S(1)}, s32[4]{0:T(128)}, u32[]{:S(2)}) %copy-start.4) | copy-done | bytes 40
  1.4 0.2 reduce-window.9
  1.6 0.1 select_reduce_fusion
  1.6 0.5 slice.12
  2.2 0.0 copy-done
  2.2 0.9 %dynamic-slice_convert_fusion = f32[256,128]{1,0:T(8,128)S(1)} fusion(bf16[256,512]{1,0:T(8,128)(2,1)} %param.6, s32[]{:T(128)S(6)} %select_n.15), kind=kLoop, calls=%fused_computation.15 | loop fusion | flops 32768 | bytes 196612 | tf_op jit(solution)/shard_map/convert_element_type | solution.py:332
  3.0 0.3 multiply_sine_fusion.1
  3.3 0.0 copy-start.3
  3.4 0.6 %fusion = (f32[256,64]{1,0:T(8,128)S(1)}, f32[256,64]{1,0:T(8,128)S(1)}, bf16[1,256,64]{2,1,0:T(8,128)(2,1)S(1)}, bf16[1,256,64]{2,1,0:T(8,128)(2,1)S(1)}, f32[256,64]{1,0:T(8,128)S(1)}) fusion(f32[64]{0:T(128)S(1)} %multiply_power_fusion, f32[256]{0:T(256)S(1)} %get-tuple-element.22, f32[256,128]{1,0:T(8,128)S(1)} %dynamic-slice_convert_fusion), kind=kLoop, calls=%fused_computation.2 | loop fusion | flops 163840 | bytes 394496 | tf_op jit(solution)/shard_map/neg | solution.py:181
  3.9 0.0 copy-start.2
  4.0 0.1 pad_maximum_fusion.1
  4.1 0.7 %pad_maximum_fusion.own_ref = bf16[2,256,128]{2,1,0:T(8,128)(2,1)} fusion(bf16[1,256,128]{2,1,0:T(8,128)(2,1)S(1)} %dynamic-slice_bitcast_fusion, bf16[1,256,64]{2,1,0:T(8,128)(2,1)S(1)} %get-tuple-element.19, bf16[1,256,64]{2,1,0:T(8,128)(2,1)S(1)} %get-tuple-element.20), kind=kLoop, calls=%fused_computation.9 | loop fusion | flops 393216 | bytes 262144 | tf_op jit(solution)/shard_map/stack | solution.py:336
  4.9 7.9 %gather_kv.1.win_ref = bf16[2,1280,128]{2,1,0:T(8,128)(2,1)} custom-call(bf16[2,256,128]{2,1,0:T(8,128)(2,1)} %pad_maximum_fusion.own_ref), custom_call_target="tpu_custom_call" | custom-call | tf_op jit(solution)/shard_map/gather_kv/pallas_call | solution.py:86
  12.8 0.0 copy-done.3
  12.8 0.0 copy-done.2
  12.8 0.0 copy-start.1
  12.8 1.1 %copy-done.1 = bf16[2,1280,128]{2,1,0:T(8,128)(2,1)S(1)} copy-done((bf16[2,1280,128]{2,1,0:T(8,128)(2,1)S(1)}, bf16[2,1280,128]{2,1,0:T(8,128)(2,1)}, u32[]{:S(2)}) %copy-start.1) | copy-done | bytes 655384
  13.9 14.4 %attend.1 = (bf16[256,2048]{1,0:T(8,128)(2,1)}, bf16[2,1024,128]{2,1,0:T(8,128)(2,1)S(1)}, f32[2,256,128]{2,1,0:T(8,128)S(1)}) custom-call(s32[1]{0:T(128)} %bitcast.3.low_ref, bf16[2,1280,128]{2,1,0:T(8,128)(2,1)S(1)} %copy-done.1, bf16[256,2048]{1,0:T(8,128)(2,1)S(1)} %copy-done.2, bf16[256,2048]{1,0:T(8,128)(2,1)S(1)} %copy-done.3, ...), custom_call_target="tpu_custom_call" | custom-call | tf_op jit(solution)/shard_map/attend/pallas_call | solution.py:187
  28.3 25.1 %scatter_grads.1 = (bf16[64,512]{1,0:T(8,128)(2,1)S(1)}, bf16[64,512]{1,0:T(8,128)(2,1)S(1)}) custom-call(bf16[2,1024,128]{2,1,0:T(8,128)(2,1)S(1)} %get-tuple-element.9.far_ref, f32[2,256,128]{2,1,0:T(8,128)S(1)} %get-tuple-element.10.own_ref, f32[256,128]{1,0:T(8,128)S(1)} %get-tuple-element.24.cos_ref, f32[256,128]{1,0:T(8,128)S(1)} %get-tuple-element.25.sin_ref), custom_call_target="tpu_custom_call" | custom-call | tf_op jit(solution)/shard_map/scatter_grads/pallas_call | solution.py:296
  53.4 0.6 %copy.10 = bf16[64,512]{1,0:T(8,128)(2,1)} copy(bf16[64,512]{1,0:T(8,128)(2,1)S(1)} %get-tuple-element.30) | data formatting | bytes 131072
  54.0 0.6 %copy.11 = bf16[64,512]{1,0:T(8,128)(2,1)} copy(bf16[64,512]{1,0:T(8,128)(2,1)S(1)} %get-tuple-element.31) | data formatting | bytes 131072
  (5 shorter events, 0.0 us)
Async XLA Ops:
  0.6 1.5 %copy-start = (bf16[256,512]{1,0:T(8,128)(2,1)S(1)}, bf16[256,512]{1,0:T(8,128)(2,1)}, u32[]{:S(2)}) copy-start(bf16[256,512]{1,0:T(8,128)(2,1)} %param.7) | copy-start | bytes 786436
  0.7 0.7 %copy-start.4 = (s32[4]{0:T(128)S(1)}, s32[4]{0:T(128)}, u32[]{:S(2)}) copy-start(s32[4]{0:T(128)} %param.9) | copy-start | bytes 52
  3.3 9.4 %copy-start.3 = (bf16[256,2048]{1,0:T(8,128)(2,1)S(1)}, bf16[256,2048]{1,0:T(8,128)(2,1)}, u32[]{:S(2)}) copy-start(bf16[256,2048]{1,0:T(8,128)(2,1)} %g_ref.1) | copy-start | bytes 3145732
  3.9 8.9 %copy-start.2 = (bf16[256,2048]{1,0:T(8,128)(2,1)S(1)}, bf16[256,2048]{1,0:T(8,128)(2,1)}, u32[]{:S(2)}) copy-start(bf16[256,2048]{1,0:T(8,128)(2,1)} %q_ref.1) | copy-start | bytes 3145732
  12.8 1.1 %copy-start.1 = (bf16[2,1280,128]{2,1,0:T(8,128)(2,1)S(1)}, bf16[2,1280,128]{2,1,0:T(8,128)(2,1)}, u32[]{:S(2)}) copy-start(bf16[2,1280,128]{2,1,0:T(8,128)(2,1)} %gather_kv.1.win_ref) | copy-start | bytes 1966084

commit v2 on v1

--- a/solution.py
+++ b/solution.py
@@ -3,6 +3,7 @@
 
 import jax
 import jax.numpy as jnp
+import numpy as np
 from jax import lax
 from jax.experimental import pallas as pl
 from jax.experimental.pallas import tpu as pltpu
@@ -21,19 +22,6 @@
 MESH = pl.DeviceIdType.MESH
 
 
-def doc_pos(doc_lengths, first, item_count):
-    starts = jnp.cumsum(doc_lengths) - doc_lengths
-    tok = first + jnp.arange(item_count, dtype=jnp.int32)
-    start_of = jnp.max(jnp.where(starts[None, :] <= tok[:, None], starts[None, :], 0), axis=1)
-    return tok, start_of, tok - start_of
-
-
-def rope_tables(pos):
-    freq = 500000.0 ** (-(2.0 * jnp.arange(HALF, dtype=jnp.float32)) / HEAD_SIZE)
-    angle = pos.astype(jnp.float32)[:, None] * freq[None, :]
-    return jnp.cos(angle), jnp.sin(angle)
-
-
 def greet(peers):
     barrier = pltpu.get_barrier_semaphore()
     count = 0
@@ -45,19 +33,41 @@
     pl.semaphore_wait(barrier, count)
 
 
-def gather_kernel(n_ctx, reach, own_ref, win_ref, send_sem, recv_sem, local_sem):
-    rows = own_ref.shape[1]
+def doc_starts(lengths_ref, tok):
+    start = jnp.int32(0)
+    found = jnp.zeros_like(tok)
+    for d in range(lengths_ref.shape[0]):
+        found = jnp.where(tok >= start, start, found)
+        start = start + lengths_ref[d]
+    return found
+
+
+def gather_kernel(
+    n_ctx, reach, heads, lengths_ref, freq_ref, keys_ref, values_ref,
+    rk_ref, v_ref, kt_ref, cos_ref, sin_ref, cos_t_ref, sin_t_ref,
+    raw, cos_all, sin_all, send_sem, recv_sem, local_sem,
+):
+    rows = keys_ref.shape[0]
     me = lax.axis_index("ctx")
     at = lax.axis_index("tp")
+    head = at * heads // QUERY_PER_KV
+    cols = pl.ds(pl.multiple_of(head * HEAD_SIZE, HEAD_SIZE), HEAD_SIZE)
+    here = pl.ds(reach * rows, rows)
+    own_key = pltpu.make_async_copy(keys_ref.at[:, cols], raw.at[0, here, :], local_sem.at[0])
+    own_value = pltpu.make_async_copy(values_ref.at[:, cols], raw.at[1, here, :], local_sem.at[1])
+    own_key.start()
+    own_value.start()
     greet(
         [(me + s < n_ctx, (lax.rem(me + s, n_ctx), at)) for s in range(1, reach + 1)]
         + [(me - s >= 0, (lax.rem(me - s + n_ctx, n_ctx), at)) for s in range(1, reach + 1)]
     )
+    own_key.wait()
+    own_value.wait()
 
     def copy(s):
         return pltpu.make_async_remote_copy(
-            src_ref=own_ref,
-            dst_ref=win_ref.at[:, pl.ds((reach - s) * rows, rows), :],
+            src_ref=raw.at[:, here, :],
+            dst_ref=raw.at[:, pl.ds((reach - s) * rows, rows), :],
             send_sem=send_sem.at[s - 1],
             recv_sem=recv_sem.at[s - 1],
             device_id=(lax.rem(me + s, n_ctx), at),
@@ -68,68 +78,130 @@
         @pl.when(me + s < n_ctx)
         def _():
             copy(s).start()
-    mine = pltpu.make_async_copy(own_ref, win_ref.at[:, pl.ds(reach * rows, rows), :], local_sem)
-    mine.start()
-    mine.wait()
+
+    freq = freq_ref[:, :1]
+    for slot in range(reach, -1, -1):
+        lanes = slice(slot * rows, (slot + 1) * rows)
+        tok = lax.broadcasted_iota(jnp.int32, (1, rows), 1) + (me - reach + slot) * rows
+        pos = (tok - doc_starts(lengths_ref, tok)).astype(jnp.float32)
+        angle = pos * freq
+        cos_all[:, lanes] = jnp.cos(angle)
+        sin_all[:, lanes] = jnp.sin(angle)
+    cos = cos_all[:, reach * rows :]
+    sin = sin_all[:, reach * rows :]
+    cos_t_ref[...] = cos
+    sin_t_ref[...] = sin
+    cos_ref[...] = jnp.concatenate([cos, cos], axis=0).T
+    sin_ref[...] = jnp.concatenate([-sin, sin], axis=0).T
+
+    def turn(slot):
+        lanes = slice(slot * rows, (slot + 1) * rows)
+        key = raw[0, lanes, :].astype(jnp.float32).T
+        one, two = key[:HALF], key[HALF:]
+        c, s = cos_all[:, lanes], sin_all[:, lanes]
+        key = jnp.concatenate([one * c - two * s, two * c + one * s], axis=0)
+        kt_ref[:, lanes] = key.astype(jnp.bfloat16)
+        rk_ref[lanes, :] = key.T.astype(jnp.bfloat16)
+        v_ref[lanes, :] = raw[1, lanes, :]
+
+    turn(reach)
     for s in range(1, reach + 1):
         @pl.when(me - s >= 0)
         def _():
             copy(s).wait_recv()
+            turn(reach - s)
     for s in range(1, reach + 1):
         @pl.when(me + s < n_ctx)
         def _():
             copy(s).wait_send()
 
 
-def gather(own, n_ctx, reach):
-    two, rows, width = own.shape
+def gather(keys, values, doc_lengths, heads, n_ctx, reach):
+    rows = keys.shape[0]
+    span = (reach + 1) * rows
+    freq = np.float32(500000.0) ** (-(2.0 * np.arange(HALF, dtype=np.float32)) / HEAD_SIZE)
+    freq = jnp.asarray(np.broadcast_to(freq.astype(np.float32)[:, None], (HALF, HEAD_SIZE)))
+    vmem = pl.BlockSpec(memory_space=pltpu.VMEM)
+    hbm = pl.BlockSpec(memory_space=pl.ANY)
     return pl.pallas_call(
-        functools.partial(gather_kernel, n_ctx, reach),
-        out_shape=jax.ShapeDtypeStruct((two, (reach + 1) * rows, width), own.dtype),
-        in_specs=[pl.BlockSpec(memory_space=pl.ANY)],
-        out_specs=pl.BlockSpec(memory_space=pl.ANY),
+        functools.partial(gather_kernel, n_ctx, reach, heads),
+        out_shape=[
+            jax.ShapeDtypeStruct((span, HEAD_SIZE), jnp.bfloat16),
+            jax.ShapeDtypeStruct((span, HEAD_SIZE), jnp.bfloat16),
+            jax.ShapeDtypeStruct((HEAD_SIZE, span), jnp.bfloat16),
+            jax.ShapeDtypeStruct((rows, HEAD_SIZE), jnp.float32),
+            jax.ShapeDtypeStruct((rows, HEAD_SIZE), jnp.float32),
+            jax.ShapeDtypeStruct((HALF, rows), jnp.float32),
+            jax.ShapeDtypeStruct((HALF, rows), jnp.float32),
+        ],
+        in_specs=[pl.BlockSpec(memory_space=pltpu.SMEM), vmem, hbm, hbm],
+        out_specs=[vmem] * 7,
         scratch_shapes=[
+            pltpu.VMEM((2, span, HEAD_SIZE), jnp.bfloat16),
+            pltpu.VMEM((HALF, span), jnp.float32),
+            pltpu.VMEM((HALF, span), jnp.float32),
             pltpu.SemaphoreType.DMA((reach,)),
             pltpu.SemaphoreType.DMA((reach,)),
-            pltpu.SemaphoreType.DMA,
+            pltpu.SemaphoreType.DMA((2,)),
         ],
-        compiler_params=pltpu.CompilerParams(collective_id=0, has_side_effects=True),
+        compiler_params=pltpu.CompilerParams(
+            collective_id=0, has_side_effects=True, vmem_limit_bytes=VMEM_LIMIT
+        ),
         name="gather_kv",
-    )(own)
+    )(doc_lengths, freq, keys, values)
 
 
 def attend_kernel(
-    reach, rows, low_ref, win_ref, q_ref, g_ref, cos_ref, sin_ref, cos_t_ref, sin_t_ref, start_ref,
-    dq_ref, far_ref, own_ref, bias, kt, dk, dv,
+    reach, rows, lengths_ref, rk_ref, v_ref, kt_ref, cos_ref, sin_ref, cos_t_ref, sin_t_ref,
+    q_ref, g_ref, dq_ref, far_ref, own_ref, bias, dk, dv, rots,
 ):
     step = pl.program_id(0)
     span = (reach + 1) * rows
+    half = rows // 2
+    first = lax.axis_index("ctx") * rows
 
     @pl.when(step == 0)
     def _():
+        query = lax.broadcasted_iota(jnp.int32, (1, rows), 1) + reach * rows
+        start = doc_starts(lengths_ref, query + (first - reach * rows)) - (first - reach * rows)
         key = lax.broadcasted_iota(jnp.int32, (span, rows), 0)
-        query = lax.broadcasted_iota(jnp.int32, (span, rows), 1) + reach * rows
-        allowed = (key >= start_ref[...]) & (key <= query)
-        bias[...] = jnp.where(allowed, 0.0, NEG)
-        kt[...] = win_ref[0].T
+        bias[...] = jnp.where((key >= start) & (key <= query), 0.0, NEG)
         dk[...] = jnp.zeros_like(dk)
         dv[...] = jnp.zeros_like(dv)
 
     nt = (((1,), (1,)), ((), ()))
-
-    def work(tiles):
-        base = span - tiles * rows
-        keys = win_ref[0, base:, :]
-        values = win_ref[1, base:, :]
+    for i in range(HEADS_PER_STEP):
+        cols = slice(i * HEAD_SIZE, (i + 1) * HEAD_SIZE)
+        raw = q_ref[:, cols].astype(jnp.float32)
+        rot = raw * cos_ref[...] + pltpu.roll(raw, HALF, 1) * sin_ref[...]
+        rots[:, cols] = rot.astype(jnp.bfloat16)
+
+    def pick(ref, side, pair):
+        return jnp.concatenate(
+            [
+                ref[side * half : (side + 1) * half, i * HEAD_SIZE : (i + 1) * HEAD_SIZE]
+                for i in (2 * pair, 2 * pair + 1)
+            ],
+            axis=0,
+        )
+
+    def twice(x):
+        return jnp.concatenate([x, x], axis=1)
+
+    def work(side, count):
+        end = span - half + side * half
+        base = end - count * half
+        keys = rk_ref[base:end, :]
+        values = v_ref[base:end, :]
+        lanes = slice(side * half, (side + 1) * half)
+        mask = twice(bias[base:end, lanes])
+        c, s = twice(cos_t_ref[:, lanes]), twice(sin_t_ref[:, lanes])
         probs, grads, dscores, queries = [], [], [], []
-        for i in range(HEADS_PER_STEP):
-            cols = slice(i * HEAD_SIZE, (i + 1) * HEAD_SIZE)
-            raw = q_ref[:, cols].astype(jnp.float32)
-            rot = raw * cos_ref[...] + pltpu.roll(raw, HALF, 1) * sin_ref[...]
-            rot = rot.astype(jnp.bfloat16)
-            grad = g_ref[:, cols]
+        for pair in range(HEADS_PER_STEP // 2):
+            rot = pick(rots, side, pair)
+            grad = pick(g_ref, side, pair)
             score = lax.dot_general(keys, rot, nt, preferred_element_type=jnp.float32)
-            score = score * (SCALE * LOG2E) + bias[base:, :]
+            score = score * (SCALE * LOG2E) + mask
             top = jnp.max(score, axis=0, keepdims=True)
             expo = jnp.exp2(score - top)
             total = jnp.sum(expo, axis=0, keepdims=True)
@@ -140,29 +212,35 @@
             probs.append(expo.astype(jnp.bfloat16))
             dscore = (expo * (dprod - delta)).astype(jnp.bfloat16)
             dscores.append(dscore)
-            spread = jnp.broadcast_to(inv, (HEAD_SIZE, rows)).T
+            spread = jnp.broadcast_to(inv, (HEAD_SIZE, 2 * half)).T
             grads.append((grad.astype(jnp.float32) * spread).astype(jnp.bfloat16))
             queries.append((rot.astype(jnp.float32) * (spread * SCALE)).astype(jnp.bfloat16))
-            dq = jnp.dot(kt[:, base:], dscore, preferred_element_type=jnp.float32)
+            dq = jnp.dot(kt_ref[:, base:end], dscore, preferred_element_type=jnp.float32)
             dq = dq * (inv * SCALE)
             one, two = dq[:HALF], dq[HALF:]
-            c, s = cos_t_ref[...], sin_t_ref[...]
             turned = jnp.concatenate([one * c + two * s, two * c - one * s], axis=0)
-            dq_ref[:, cols] = turned.T.astype(jnp.bfloat16)
-        dv[base:, :] += jnp.dot(
+            turned = turned.astype(jnp.bfloat16).T
+            for i in range(2):
+                at = (2 * pair + i) * HEAD_SIZE
+                dq_ref[lanes, at : at + HEAD_SIZE] = turned[i * half : (i + 1) * half, :]
+        dv[base:end, :] += jnp.dot(
             jnp.concatenate(probs, axis=1), jnp.concatenate(grads, axis=0),
             preferred_element_type=jnp.float32,
         )
-        dk[base:, :] += jnp.dot(
+        dk[base:end, :] += jnp.dot(
             jnp.concatenate(dscores, axis=1), jnp.concatenate(queries, axis=0),
             preferred_element_type=jnp.float32,
         )
 
-    tiles = reach + 1 - low_ref[0] // rows
-    for count in range(1, reach + 2):
-        @pl.when(tiles == count)
-        def _():
-            work(count)
+    for side in range(2):
+        tok = first + side * half
+        low = doc_starts(lengths_ref, tok) - (first - reach * rows)
+        most = 2 * reach + 1 + side
+        tiles = most - low // half
+        for count in range(1, most + 1):
+            @pl.when(tiles == count)
+            def _():
+                work(side, count)
 
     @pl.when(step == pl.num_programs(0) - 1)
     def _():
@@ -172,13 +250,10 @@
         own_ref[1] = dv[reach * rows :, :]
 
 
-def attend(window, queries, grad_out, low, start_row, cos, sin, reach):
+def attend(window, queries, grad_out, doc_lengths, reach):
     rows, width = queries.shape
     span = (reach + 1) * rows
     block = HEADS_PER_STEP * HEAD_SIZE
-    steps = width // block
-    cos_wide = jnp.concatenate([cos, cos], axis=1)
-    sin_wide = jnp.concatenate([-sin, sin], axis=1)
 
     def whole(shape):
         return pl.BlockSpec(shape, lambda i, low: (0,) * len(shape))
@@ -188,20 +263,16 @@
         functools.partial(attend_kernel, reach, rows),
         grid_spec=pltpu.PrefetchScalarGridSpec(
             num_scalar_prefetch=1,
-            grid=(steps,),
-            in_specs=[
-                whole((2, span, HEAD_SIZE)), by_head, by_head,
-                whole((rows, HEAD_SIZE)), whole((rows, HEAD_SIZE)),
-                whole((HALF, rows)), whole((HALF, rows)), whole((1, rows)),
-            ],
+            grid=(width // block,),
+            in_specs=[whole(x.shape) for x in window] + [by_head, by_head],
             out_specs=[
                 by_head, whole((2, reach * rows, HEAD_SIZE)), whole((2, rows, HEAD_SIZE)),
             ],
             scratch_shapes=[
                 pltpu.VMEM((span, rows), jnp.float32),
-                pltpu.VMEM((HEAD_SIZE, span), jnp.bfloat16),
                 pltpu.VMEM((span, HEAD_SIZE), jnp.float32),
                 pltpu.VMEM((span, HEAD_SIZE), jnp.float32),
+                pltpu.VMEM((rows, block), jnp.bfloat16),
             ],
         ),
         out_shape=[
@@ -213,7 +284,7 @@
             dimension_semantics=("arbitrary",), vmem_limit_bytes=VMEM_LIMIT
         ),
         name="attend",
-    )(low, window, queries, grad_out, cos_wide, sin_wide, cos.T, sin.T, start_row)
+    )(doc_lengths, *window, queries, grad_out)
 
 
 def scatter_kernel(
@@ -320,24 +391,11 @@
     heads = queries.shape[1] // HEAD_SIZE
     n_ctx = lax.axis_size("ctx")
     n_tp = lax.axis_size("tp")
-    at = lax.axis_index("tp")
-    head = at * heads // QUERY_PER_KV
     share = max(1, QUERY_PER_KV // heads)
     reach = min(-(-MAXDOC // rows), n_ctx - 1)
-    first = lax.axis_index("ctx") * rows
-    tok, start_of, pos = doc_pos(doc_lengths, first, rows)
-    cos, sin = rope_tables(pos)
-    start_row = (start_of - (first - reach * rows))[None, :]
-    low = start_row[0, :1]
-    key = lax.dynamic_slice_in_dim(keys, head * HEAD_SIZE, HEAD_SIZE, 1).astype(jnp.float32)
-    value = lax.dynamic_slice_in_dim(values, head * HEAD_SIZE, HEAD_SIZE, 1)
-    one, two = key[:, :HALF], key[:, HALF:]
-    key = jnp.concatenate([one * cos - two * sin, two * cos + one * sin], axis=1)
-    own = jnp.stack([key.astype(jnp.bfloat16), value])
-    window = gather(own, n_ctx, reach)
-    grad_queries, far, near = attend(window, queries, grad_out, low, start_row, cos, sin, reach)
-    cos_wide = jnp.concatenate([cos, cos], axis=1)
-    sin_wide = jnp.concatenate([-sin, sin], axis=1)
+    window = gather(keys, values, doc_lengths, heads, n_ctx, reach)
+    cos_wide, sin_wide = window[3], window[4]
+    grad_queries, far, near = attend(window, queries, grad_out, doc_lengths, reach)
     keys_gradient, values_gradient = scatter(
         far, near, cos_wide, sin_wide, n_ctx, n_tp, reach, share
     )

time: 55.2 us -> 55.9 us (1.013)
  other arithmetic: 2.92 us -> 0 us
  local copies, waits for them, and re-layouts: 3.56 us -> 6.35 us
  Pallas kernels: 47.4 us -> 48.6 us
    unnamed x12, local copies, waits for them, and re-layouts: 3.03 us -> 5.61 us
    pallas_call x1, Pallas kernels: 14.4 us -> 15.6 us  [attend(): pl.pallas_call(functools.partial(attend_kernel, reach, rows), grid_spec=p...]
    another operation x2 -> x0, other arithmetic: 0.93 us -> none  [the longest x1 0.75 us: local(): own = jnp.stack([key.astype(jnp.bfloat16), value])]
    convert_element_type x2 -> x0, other arithmetic: 0.87 us -> none  [the longest x1 0.86 us: local(): lax.dynamic_slice_in_dim(keys, head * HEAD_SIZE, HEAD_SIZE, 1)]
    another operation x1, local copies, waits for them, and re-layouts: 0.01 us -> 0.73 us  [local(): own = jnp.stack([key.astype(jnp.bfloat16), value])]
    neg x1 -> x0, other arithmetic: 0.58 us -> none  [attend(): sin_wide = jnp.concatenate([-sin, sin], axis=1)]
where the time goes in v2:
time: 55.9 us; the launch traced here: 55.6 us
  Pallas kernels  48.6 us (87%)
  local copies, waits for them, and re-layouts  6.35 us (11%)
  between operations  0.67 us (1%)
    pallas_call x1, Pallas kernels, scatter(): pl.pallas_call(functools.partial(scatter_kernel, n_ctx, n_tp, reach, shar...  24.8 us
    pallas_call x1, Pallas kernels, attend(): pl.pallas_call(functools.partial(attend_kernel, reach, rows), grid_spec=p...  15.6 us
    pallas_call x1, Pallas kernels, gather(): pl.pallas_call(functools.partial(gather_kernel, n_ctx, reach, heads), out...  8.16 us
    unnamed x12, local copies, waits for them, and re-layouts  5.61 us

profile of v2, /device:TPU:3, one launch (start us, length us, event | category | flops | bytes accessed | tf_op | source)
XLA Modules:
  0.0 55.6 jit_solution(8596066329642528966)
XLA Ops:
  0.6 0.0 copy-start.4
  0.6 0.7 %jit_solution_.3.freq_ref = f32[64,128]{1,0:T(8,128)S(1)} broadcast(f32[64]{0:T(128)} %constant.2.clone), dimensions={0} | broadcast | bytes 33024 | tf_op jit(solution)
  1.4 0.0 copy-done.4
  1.4 0.0 copy-start.2
  1.4 1.0 %copy-done.2 = bf16[256,512]{1,0:T(8,128)(2,1)S(1)} copy-done((bf16[256,512]{1,0:T(8,128)(2,1)S(1)}, bf16[256,512]{1,0:T(8,128)(2,1)}, u32[]{:S(2)}) %copy-start.2) | copy-done | bytes 262168
  2.3 0.0 copy-start.3
  2.3 0.9 %copy-done.3 = bf16[256,512]{1,0:T(8,128)(2,1)S(1)} copy-done((bf16[256,512]{1,0:T(8,128)(2,1)S(1)}, bf16[256,512]{1,0:T(8,128)(2,1)}, u32[]{:S(2)}) %copy-start.3) | copy-done | bytes 262168
  3.3 8.2 %gather_kv.1 = (bf16[1280,128]{1,0:T(8,128)(2,1)S(1)}, bf16[1280,128]{1,0:T(8,128)(2,1)S(1)}, bf16[128,1280]{1,0:T(8,128)(2,1)S(1)}, f32[256,128]{1,0:T(8,128)S(...) custom-call(s32[4]{0:T(128)S(1)} %copy-done.4, f32[64,128]{1,0:T(8,128)S(1)} %jit_solution_.3.freq_ref, ...), custom_call_target="tpu_custom_call" | custom-call | tf_op jit(solution)/shard_map/gather_kv/pallas_call | solution.py:126
  11.4 0.0 copy-start
  11.5 1.2 %copy-done = bf16[256,2048]{1,0:T(8,128)(2,1)S(1)} copy-done((bf16[256,2048]{1,0:T(8,128)(2,1)S(1)}, bf16[256,2048]{1,0:T(8,128)(2,1)}, u32[]{:S(2)}) %copy-start) | copy-done | bytes 1048600
  12.7 0.0 copy-start.1
  12.7 1.2 %copy-done.1 = bf16[256,2048]{1,0:T(8,128)(2,1)S(1)} copy-done((bf16[256,2048]{1,0:T(8,128)(2,1)S(1)}, bf16[256,2048]{1,0:T(8,128)(2,1)}, u32[]{:S(2)}) %copy-start.1) | copy-done | bytes 1048600
  13.9 15.6 %attend.1 = (bf16[256,2048]{1,0:T(8,128)(2,1)}, bf16[2,1024,128]{2,1,0:T(8,128)(2,1)S(1)}, f32[2,256,128]{2,1,0:T(8,128)S(1)}) custom-call(s32[4]{0:T(128)S(1)} %copy-done.4, bf16[1280,128]{1,0:T(8,128)(2,1)S(1)} %get-tuple-element.15.rk_ref, bf16[1280,128]{1,0:T(8,128)(2,1)S(1)} %get-tuple-element.16.v_ref, bf16[128,1280]{1,0:T(8,128)(2,1)S(1)} %get-tuple-element.17.kt_ref, ...), custom_call_target="tpu_custom_call" | custom-call | tf_op jit(solution)/shard_map/attend/pallas_call | solution.py:262
  29.5 24.8 %scatter_grads.1 = (bf16[64,512]{1,0:T(8,128)(2,1)S(1)}, bf16[64,512]{1,0:T(8,128)(2,1)S(1)}) custom-call(bf16[2,1024,128]{2,1,0:T(8,128)(2,1)S(1)} %get-tuple-element.23.far_ref, f32[2,256,128]{2,1,0:T(8,128)S(1)} %get-tuple-element.24.own_ref, f32[256,128]{1,0:T(8,128)S(1)} %get-tuple-element.18.cos_ref, f32[256,128]{1,0:T(8,128)S(1)} %get-tuple-element.19.sin_ref), custom_call_target="tpu_custom_call" | custom-call | tf_op jit(solution)/shard_map/scatter_grads/pallas_call | solution.py:367
  54.3 0.6 %copy.11 = bf16[64,512]{1,0:T(8,128)(2,1)} copy(bf16[64,512]{1,0:T(8,128)(2,1)S(1)} %get-tuple-element.31) | data formatting | bytes 131072
  55.0 0.6 %copy.12 = bf16[64,512]{1,0:T(8,128)(2,1)} copy(bf16[64,512]{1,0:T(8,128)(2,1)S(1)} %get-tuple-element.32) | data formatting | bytes 131072
Async XLA Ops:
  0.6 0.7 %copy-start.4 = (s32[4]{0:T(128)S(1)}, s32[4]{0:T(128)}, u32[]{:S(2)}) copy-start(s32[4]{0:T(128)} %lengths_ref.3) | copy-start | bytes 52
  1.4 1.0 %copy-start.2 = (bf16[256,512]{1,0:T(8,128)(2,1)S(1)}, bf16[256,512]{1,0:T(8,128)(2,1)}, u32[]{:S(2)}) copy-start(bf16[256,512]{1,0:T(8,128)(2,1)} %keys_ref.1) | copy-start | bytes 786436
  2.3 0.9 %copy-start.3 = (bf16[256,512]{1,0:T(8,128)(2,1)S(1)}, bf16[256,512]{1,0:T(8,128)(2,1)}, u32[]{:S(2)}) copy-start(bf16[256,512]{1,0:T(8,128)(2,1)} %values_ref.1) | copy-start | bytes 786436
  11.4 1.2 %copy-start = (bf16[256,2048]{1,0:T(8,128)(2,1)S(1)}, bf16[256,2048]{1,0:T(8,128)(2,1)}, u32[]{:S(2)}) copy-start(bf16[256,2048]{1,0:T(8,128)(2,1)} %q_ref.1) | copy-start | bytes 3145732
  12.7 1.2 %copy-start.1 = (bf16[256,2048]{1,0:T(8,128)(2,1)S(1)}, bf16[256,2048]{1,0:T(8,128)(2,1)}, u32[]{:S(2)}) copy-start(bf16[256,2048]{1,0:T(8,128)(2,1)} %g_ref.1) | copy-start | bytes 3145732

commit v3 on v2

--- a/solution.py
+++ b/solution.py
@@ -3,7 +3,6 @@
 
 import jax
 import jax.numpy as jnp
-import numpy as np
 from jax import lax
 from jax.experimental import pallas as pl
 from jax.experimental.pallas import tpu as pltpu
@@ -17,8 +16,8 @@
 HALF = HEAD_SIZE // 2
 SCALE = HEAD_SIZE ** (-0.5)
 LOG2E = math.log2(math.e)
-HEADS_PER_STEP = 2
-VMEM_LIMIT = 48 << 20
+HEADS_PER_STEP = 4
+VMEM_LIMIT = 60 << 20
 MESH = pl.DeviceIdType.MESH
 
 
@@ -43,7 +42,7 @@
 
 
 def gather_kernel(
-    n_ctx, reach, heads, lengths_ref, freq_ref, keys_ref, values_ref,
+    n_ctx, reach, heads, lengths_ref, keys_ref, values_ref,
     rk_ref, v_ref, kt_ref, cos_ref, sin_ref, cos_t_ref, sin_t_ref,
     raw, cos_all, sin_all, send_sem, recv_sem, local_sem,
 ):
@@ -79,7 +78,8 @@
         def _():
             copy(s).start()
 
-    freq = freq_ref[:, :1]
+    index = lax.broadcasted_iota(jnp.int32, (HALF, HEAD_SIZE), 0).astype(jnp.float32)
+    freq = jnp.exp2(index * (-2.0 / HEAD_SIZE * math.log2(500000.0)))[:, :1]
     for slot in range(reach, -1, -1):
         lanes = slice(slot * rows, (slot + 1) * rows)
         tok = lax.broadcasted_iota(jnp.int32, (1, rows), 1) + (me - reach + slot) * rows
@@ -119,10 +119,8 @@
 def gather(keys, values, doc_lengths, heads, n_ctx, reach):
     rows = keys.shape[0]
     span = (reach + 1) * rows
-    freq = np.float32(500000.0) ** (-(2.0 * np.arange(HALF, dtype=np.float32)) / HEAD_SIZE)
-    freq = jnp.asarray(np.broadcast_to(freq.astype(np.float32)[:, None], (HALF, HEAD_SIZE)))
     vmem = pl.BlockSpec(memory_space=pltpu.VMEM)
-    hbm = pl.BlockSpec(memory_space=pl.ANY)
+    hbm = pl.BlockSpec(memory_space=pltpu.HBM)
     return pl.pallas_call(
         functools.partial(gather_kernel, n_ctx, reach, heads),
         out_shape=[
@@ -134,7 +132,7 @@
             jax.ShapeDtypeStruct((HALF, rows), jnp.float32),
             jax.ShapeDtypeStruct((HALF, rows), jnp.float32),
         ],
-        in_specs=[pl.BlockSpec(memory_space=pltpu.SMEM), vmem, hbm, hbm],
+        in_specs=[pl.BlockSpec(memory_space=pltpu.SMEM), hbm, hbm],
         out_specs=[vmem] * 7,
         scratch_shapes=[
             pltpu.VMEM((2, span, HEAD_SIZE), jnp.bfloat16),
@@ -148,7 +146,7 @@
             collective_id=0, has_side_effects=True, vmem_limit_bytes=VMEM_LIMIT
         ),
         name="gather_kv",
-    )(doc_lengths, freq, keys, values)
+    )(doc_lengths, keys, values)
 
 
 def attend_kernel(

time: 55.9 us -> 55.7 us (level); the launches traced: 55.6 us -> 56.6 us
  Pallas kernels: 48.6 us -> 53.8 us
  local copies, waits for them, and re-layouts: 6.35 us -> 2.14 us
    pallas_call x1, Pallas kernels: 24.8 us -> 28.4 us  [scatter(): pl.pallas_call(functools.partial(scatter_kernel, n_ctx, n_tp, reach, shar...]
    unnamed x12 -> x4, local copies, waits for them, and re-layouts: 5.61 us -> 2.14 us
    pallas_call x1, Pallas kernels: 8.16 us -> 9.39 us  [gather(): pl.pallas_call(functools.partial(gather_kernel, n_ctx, reach, heads), out...]
    another operation x1 -> x0, local copies, waits for them, and re-layouts: 0.73 us -> none
where the time goes in v3:
time: 55.7 us; the launch traced here: 56.6 us
  Pallas kernels  53.8 us (97%)
  local copies, waits for them, and re-layouts  2.14 us (4%)
  between operations  0.66 us (1%)
    pallas_call x1, Pallas kernels, scatter(): pl.pallas_call(functools.partial(scatter_kernel, n_ctx, n_tp, reach, shar...  28.4 us
    pallas_call x1, Pallas kernels, attend(): pl.pallas_call(functools.partial(attend_kernel, reach, rows), grid_spec=p...  16 us
    pallas_call x1, Pallas kernels, gather(): pl.pallas_call(functools.partial(gather_kernel, n_ctx, reach, heads), out...  9.39 us
    unnamed x4, local copies, waits for them, and re-layouts  2.14 us

profile of v3, /device:TPU:3, one launch (start us, length us, event | category | flops | bytes accessed | tf_op | source)
XLA Modules:
  0.0 56.6 jit_solution(1979739333648737114)
XLA Ops:
  0.6 9.4 %gather_kv.1 = (bf16[1280,128]{1,0:T(8,128)(2,1)}, bf16[1280,128]{1,0:T(8,128)(2,1)}, bf16[128,1280]{1,0:T(8,128)(2,1)}, f32[256,128]{1,0:T(8,128)}, f32[256,128...) custom-call(s32[4]{0:T(128)} %lengths_ref.3, bf16[256,512]{1,0:T(8,128)(2,1)} %keys_ref.1, bf16[256,512]{1,0:T(8,128)(2,1)} %values_ref.1), custom_call_target="tpu_custom_call" | custom-call | tf_op jit(solution)/shard_map/gather_kv/pallas_call | solution.py:124
  10.0 16.0 %attend.1 = (bf16[256,2048]{1,0:T(8,128)(2,1)}, bf16[2,1024,128]{2,1,0:T(8,128)(2,1)}, f32[2,256,128]{2,1,0:T(8,128)}) custom-call(s32[4]{0:T(128)} %lengths_ref.3, bf16[1280,128]{1,0:T(8,128)(2,1)} %get-tuple-element.15.rk_ref, bf16[1280,128]{1,0:T(8,128)(2,1)} %get-tuple-element.16.v_ref, bf16[128,1280]{1,0:T(8,128)(2,1)} %get-tuple-element.17.kt_ref, ...), custom_call_target="tpu_custom_call" | custom-call | tf_op jit(solution)/shard_map/attend/pallas_call | solution.py:260
  26.0 28.4 %scatter_grads.1 = (bf16[64,512]{1,0:T(8,128)(2,1)}, bf16[64,512]{1,0:T(8,128)(2,1)}) custom-call(bf16[2,1024,128]{2,1,0:T(8,128)(2,1)} %get-tuple-element.23.far_ref, f32[2,256,128]{2,1,0:T(8,128)} %get-tuple-element.24.own_ref, f32[256,128]{1,0:T(8,128)} %get-tuple-element.18.cos_ref, f32[256,128]{1,0:T(8,128)} %get-tuple-element.19.sin_ref), custom_call_target="tpu_custom_call" | custom-call | tf_op jit(solution)/shard_map/scatter_grads/pallas_call | solution.py:365
  54.5 0.0 copy-start
  54.5 1.5 %copy.10 = bf16[64,512]{1,0:T(8,128)(2,1)} copy(bf16[64,512]{1,0:T(8,128)(2,1)} %get-tuple-element.31) | data formatting | bytes 131072
  56.0 0.0 copy-done
  56.0 0.6 %copy.11 = bf16[64,512]{1,0:T(8,128)(2,1)} copy(bf16[64,512]{1,0:T(8,128)(2,1)S(1)} %copy-done) | data formatting | bytes 131072
Async XLA Ops:
  54.5 1.5 %copy-start = (bf16[64,512]{1,0:T(8,128)(2,1)S(1)}, bf16[64,512]{1,0:T(8,128)(2,1)}, u32[]{:S(2)}) copy-start(bf16[64,512]{1,0:T(8,128)(2,1)} %get-tuple-element.32) | copy-start | bytes 196612
